TPU v7x, 256 devices: a whole 4x4x8 slice. The times are simulated.
256 devices in a mesh: seg: 16 (over z, core), bond: 16 (over x, y).
Axes of the slice: x: 4, y: 4, z: 8, core: 2. Of those that a mesh axis runs over, the one named last changes fastest.
Arguments:
- left_env: bfloat16 [16, 1024, 6, 1024], P('seg', 'bond'), may hold values from -0.1875 to 0.1875
- prev_left: bfloat16 [16, 1024, 1024], P('seg'), may hold values from -0.25 to 1.25
- cur_site: bfloat16 [16, 1024, 4, 1024], P('seg', 'bond'), may hold values from -6 to 6
- prev_site: bfloat16 [16, 1024, 4, 1024], P('seg', None, None, 'bond'), may hold values from -6 to 6
- hamiltonian: bfloat16 [16, 6, 6, 4, 4], P('seg'), may hold values from -1.25 to 1.25
- right_env: bfloat16 [16, 1024, 6, 1024], P('seg', 'bond'), may hold values from -0.078125 to 0.078125
- prev_right: bfloat16 [16, 1024, 1024], P('seg'), may hold values from -0.25 to 1.25
Outputs:
- new_site: bfloat16 [16, 1024, 4, 1024], P('seg', 'bond')
- center: float32 [16, 1024, 1024], P('seg', 'bond')
All inputs are finite; a program needn't handle non-finite values.
Results may differ from a plain program's by a relative error of at most 0.0054.
Values may be sent and summed in bfloat16 or wider, within the bound.
No kernel may reach another device: no remote copies, remote signals or barrier semaphores. Data moves between devices by JAX's collectives and lax.ppermute only.
A program may use at most 128 MiB of HBM per device.

v0:
```python
import math
import jax
import jax.numpy as jnp
from jax import lax
from jax.sharding import PartitionSpec as P

PHYS = 4
MPOB = 6


def shifted(block, axis, distance):
    devices = range(lax.axis_size(axis))
    route = [((i - distance) % len(devices), i) for i in devices]
    return lax.ppermute(block, axis, route)


def shards(left_env, prev_left, cur_site, prev_site, hamiltonian, right_env, prev_right):
    left_now, prev_now = shifted((left_env[0], prev_left[0]), "seg", 1)
    own_rows = left_now.shape[0]
    bond_width = left_now.shape[2]
    coupling = hamiltonian[0].astype(jnp.float32)
    current = lax.all_gather(cur_site[0], "bond", axis=0, tiled=True)
    projected = jnp.dot(
        left_now.reshape(own_rows * MPOB, bond_width),
        current.reshape(bond_width, PHYS * bond_width),
        preferred_element_type=jnp.float32,
    ).reshape(own_rows, MPOB, PHYS, bond_width)
    mixture = jnp.einsum(
        "autc,uvst->asvc", projected, coupling, precision=lax.Precision.HIGHEST
    ).astype(jnp.bfloat16)
    applied = jnp.einsum(
        "asvc,cvy->asy",
        mixture,
        lax.all_gather(right_env[0], "bond", axis=0, tiled=True),
        preferred_element_type=jnp.float32,
    )
    previous = lax.all_gather(prev_site[0], "bond", axis=2, tiled=True)
    own_left = lax.dynamic_slice_in_dim(prev_now, lax.axis_index("bond") * own_rows, own_rows, 0)
    partial_value = jnp.einsum(
        "ab,bsc->asc", own_left, previous, preferred_element_type=jnp.float32
    ).astype(jnp.bfloat16)
    second = jnp.einsum(
        "asc,cy->asy", partial_value, prev_right[0], preferred_element_type=jnp.float32
    )
    target = (2.0 * applied - second).reshape(own_rows * PHYS, bond_width)
    local_correlation = jnp.dot(
        target.T, target, precision=lax.Precision.HIGHEST, preferred_element_type=jnp.float32
    )
    correlation = lax.psum(local_correlation, "bond")
    triangle = jnp.linalg.cholesky(correlation)
    solved = jax.scipy.linalg.solve_triangular(triangle, target.T, lower=True)
    norming = math.sqrt(bond_width * PHYS)
    new_site = (solved.T * norming).astype(jnp.bfloat16).reshape(1, own_rows, PHYS, bond_width)
    offset = lax.axis_index("bond") * own_rows
    center = lax.dynamic_slice_in_dim(triangle.T, offset, own_rows, 0) / norming
    return (new_site, center[None])


def solution(mesh):
    return jax.shard_map(
        shards,
        mesh=mesh,
        in_specs=(
            P("seg", "bond", None, None),
            P("seg", None, None),
            P("seg", "bond", None, None),
            P("seg", None, None, "bond"),
            P("seg", None, None, None, None),
            P("seg", "bond", None, None),
            P("seg", None, None),
        ),
        out_specs=(P("seg", "bond", None, None), P("seg", "bond", None)),
        check_vma=False,
    )
```

profile of v0, /device:TPU:1, one launch (start us, length us, event | category | flops | bytes accessed | tf_op | source)
XLA Modules:
  0.0 756.7 jit_solution(14787921494383537855)
XLA Ops:
  14.1 75.9 %all-gather.7.cloned.1.call-done = bf16[1,1024,4,1024]{3,2,0,1:T(4,128)(2,1)} async-done(((bf16[1,64,4,1024]{3,2,0,1:T(4,128)(2,1)}), bf16[1,1024,4,1024]{3,2,0,1:T(4,128)(2,1)}) %all-gather.7.cloned.1.call-update) | async-done | bytes 8388624 | tf_op jit(solution)/shard_map/all_gather | solution.py:22
  90.0 13.8 %copy.82 = bf16[1,1024,4,1024]{1,3,2,0:T(8,128)(2,1)} copy(bf16[1,1024,4,1024]{3,2,0,1:T(4,128)(2,1)} %all-gather.7.cloned.1.call-done) | data formatting | bytes 16777216 | tf_op jit(solution)/shard_map/reshape | solution.py:25
  103.9 64.7 %all-gather.11.cloned.1.call-done = bf16[1,1024,4,1024]{1,2,0,3:T(4,128)(2,1)} async-done(((bf16[1,1024,4,64]{1,2,0,3:T(4,128)(2,1)}), bf16[1,1024,4,1024]{1,2,0,3:T(4,128)(2,1)}) %all-gather.11.cloned.1.call-update) | async-done | bytes 8388624 | tf_op jit(solution)/shard_map/all_gather | solution.py:37
  168.6 13.7 %copy.57 = bf16[1,1024,4,1024]{3,1,2,0:T(8,128)(2,1)} copy(bf16[1,1024,4,1024]{1,2,0,3:T(4,128)(2,1)} %all-gather.11.cloned.1.call-done) | data formatting | bytes 16777216 | tf_op jit(solution)/shard_map/all_gather | solution.py:37
  188.6 11.5 %fusion.8 = bf16[64,4,6,1024]{3,2,1,0:T(8,128)(2,1)} fusion(f32[64,6,4,1024,1]{3,0,2,1,4:T(8,128)S(1)} %fusion.14, bf16[1,6,6,4,4]{2,4,3,1,0:T(4,128)(2,1)S(1)} %copy-done.4), kind=kOutput, calls=%fused_computation.11 | convolution fusion | flops 454557696 | bytes 9438336 | tf_op jit(solution)/shard_map/autc,uvst->asvc/dot_general | solution.py:28
  200.2 65.7 %all-gather.9.cloned.1.call-done = bf16[1,1024,6,1024]{3,1,2,0:T(8,128)(2,1)} async-done(((bf16[1,64,6,1024]{3,1,2,0:T(8,128)(2,1)}), bf16[1,1024,6,1024]{3,1,2,0:T(8,128)(2,1)}) %all-gather.9.cloned.1.call-update) | async-done | bytes 12582928 | tf_op jit(solution)/shard_map/all_gather | solution.py:34
  265.9 12.8 %fusion.24 = f32[64,4,1024]{2,0,1:T(8,128)} fusion(bf16[1,1024,6,1024]{3,1,2,0:T(8,128)(2,1)} %all-gather.9.cloned.1.call-done, bf16[64,4,6,1024]{3,2,1,0:T(8,128)(2,1)} %fusion.8), kind=kOutput, calls=%fused_computation.23 | convolution fusion | flops 3221487616 | bytes 16777216 | tf_op jit(solution)/shard_map/asvc,cvy->asy/dot_general | solution.py:31
  291.1 111.9 %all-reduce.3.cloned.1.call-done = f32[1024,1024]{0,1:T(8,128)} async-done(((f32[1024,1024]{0,1:T(8,128)}), f32[1024,1024]{0,1:T(8,128)}) %all-reduce.3.cloned.1.call-update) | async-done | bytes 4194320 | tf_op jit(solution)/shard_map/psum | solution.py:49
  414.9 11.7 %cholesky.223 = f32[128,128]{1,0:T(8,128)S(1)} custom-call(f32[128,128]{1,0:T(8,128)S(1)} %cholesky.580), custom_call_target="Cholesky" | custom-call | tf_op jit(solution)/shard_map/jit(cholesky)/cholesky | solution.py:50
  426.6 9.8 %custom-call.63 = f32[1,128,128]{1,2,0:T(8,128)S(1)} custom-call(f32[1,128,128]{2,1,0:T(8,128)S(1)} %get-tuple-element.76), custom_call_target="InvertDiagBlocksLowerTriangular" | custom-call | tf_op jit(solution)/shard_map/jit(cholesky)/cholesky | solution.py:50
  442.7 11.9 %cholesky.244 = f32[128,128]{1,0:T(8,128)S(1)} custom-call(f32[128,128]{1,0:T(8,128)S(1)} %cholesky.584), custom_call_target="Cholesky" | custom-call | tf_op jit(solution)/shard_map/jit(cholesky)/cholesky | solution.py:50
  456.1 9.8 %custom-call.64 = f32[1,128,128]{1,2,0:T(8,128)S(1)} custom-call(f32[1,128,128]{2,1,0:T(8,128)S(1)} %get-tuple-element.73), custom_call_target="InvertDiagBlocksLowerTriangular" | custom-call | tf_op jit(solution)/shard_map/jit(cholesky)/cholesky | solution.py:50
  469.3 11.7 %cholesky.468 = f32[128,128]{1,0:T(8,128)S(1)} custom-call(f32[128,128]{1,0:T(8,128)S(1)} %cholesky.589), custom_call_target="Cholesky" | custom-call | tf_op jit(solution)/shard_map/jit(cholesky)/cholesky | solution.py:50
  482.3 9.8 %custom-call.65 = f32[1,128,128]{1,2,0:T(8,128)S(1)} custom-call(f32[1,128,128]{2,1,0:T(8,128)S(1)} %get-tuple-element.70), custom_call_target="InvertDiagBlocksLowerTriangular" | custom-call | tf_op jit(solution)/shard_map/jit(cholesky)/cholesky | solution.py:50
  495.6 12.1 %cholesky.487 = f32[128,128]{1,0:T(8,128)S(1)} custom-call(f32[128,128]{1,0:T(8,128)S(1)} %cholesky.594), custom_call_target="Cholesky" | custom-call | tf_op jit(solution)/shard_map/jit(cholesky)/cholesky | solution.py:50
  509.0 9.8 %custom-call.66 = f32[1,128,128]{1,2,0:T(8,128)S(1)} custom-call(f32[1,128,128]{2,1,0:T(8,128)S(1)} %get-tuple-element.67), custom_call_target="InvertDiagBlocksLowerTriangular" | custom-call | tf_op jit(solution)/shard_map/jit(cholesky)/cholesky | solution.py:50
  522.3 11.7 %cholesky.506 = f32[128,128]{1,0:T(8,128)S(1)} custom-call(f32[128,128]{1,0:T(8,128)S(1)} %cholesky.599), custom_call_target="Cholesky" | custom-call | tf_op jit(solution)/shard_map/jit(cholesky)/cholesky | solution.py:50
  535.4 10.0 %custom-call.67 = f32[1,128,128]{1,2,0:T(8,128)S(1)} custom-call(f32[1,128,128]{2,1,0:T(8,128)S(1)} %get-tuple-element.64), custom_call_target="InvertDiagBlocksLowerTriangular" | custom-call | tf_op jit(solution)/shard_map/jit(cholesky)/cholesky | solution.py:50
  548.7 11.7 %cholesky.526 = f32[128,128]{1,0:T(8,128)S(1)} custom-call(f32[128,128]{1,0:T(8,128)S(1)} %cholesky.604), custom_call_target="Cholesky" | custom-call | tf_op jit(solution)/shard_map/jit(cholesky)/cholesky | solution.py:50
  574.5 11.9 %cholesky.546 = f32[128,128]{1,0:T(8,128)S(1)} custom-call(f32[128,128]{1,0:T(8,128)S(1)} %cholesky.609), custom_call_target="Cholesky" | custom-call | tf_op jit(solution)/shard_map/jit(cholesky)/cholesky | solution.py:50
  587.6 9.8 %custom-call.69 = f32[1,128,128]{1,2,0:T(8,128)S(1)} custom-call(f32[1,128,128]{2,1,0:T(8,128)S(1)} %get-tuple-element.58), custom_call_target="InvertDiagBlocksLowerTriangular" | custom-call | tf_op jit(solution)/shard_map/jit(cholesky)/cholesky | solution.py:50
  600.1 11.7 %cholesky.564 = f32[128,128]{1,0:T(8,128)S(1)} custom-call(f32[128,128]{1,0:T(8,128)S(1)} %convolution_subtract_fusion.13), custom_call_target="Cholesky" | custom-call | tf_op jit(solution)/shard_map/jit(cholesky)/cholesky | solution.py:50
  625.3 27.4 %while.1 = (s32[]{:T(128)}, f32[1024,1024]{1,0:T(8,128)}, s32[8,2]{0,1:T(2,128)S(1)}, f32[8,128,128]{2,1,0:T(8,128)}, s32[]{:T(128)}) while((s32[]{:T(128)}, f32[1024,1024]{1,0:T(8,128)}, s32[8,2]{0,1:T(2,128)S(1)}, f32[8,128,128]{2,1,0:T(8,128)}, s32[]{:T(128)}) %tuple.65), condition=%wide.while_cond, body=%wide.while_body.sunk | while | flops 2 | bytes 132705 | solution.py:51
  652.7 79.6 %custom-call.70 = f32[8,128,128]{1,2,0:T(8,128)S(1)} custom-call(f32[8,128,128]{2,1,0:T(8,128)} %get-tuple-element.9), custom_call_target="InvertDiagBlocksLowerTriangular" | custom-call | tf_op jit(solution)/shard_map/jit(_solve_triangular)/triangular_solve | solution.py:51
  (119 shorter events, 134.0 us)
Async XLA Ops:
  7.2 271.5 %copy-start = (bf16[1,1024,1024]{2,1,0:T(8,128)(2,1)S(1)}, bf16[1,1024,1024]{2,1,0:T(8,128)(2,1)}, u32[]{:S(2)}) copy-start(bf16[1,1024,1024]{2,1,0:T(8,128)(2,1)} %param.13) | copy-start | bytes 6291460
  7.2 82.9 %all-gather.7.cloned.1.call-start = ((), (), s32[]{:S(2)}) async-start(), calls=%async_computation.1 | async-start | bytes 8912896 | tf_op jit(solution)/shard_map/all_gather | solution.py:22
  7.9 160.7 %all-gather.11.cloned.1.call-start = ((), (), s32[]{:S(2)}) async-start(), calls=%async_computation.3 | async-start | bytes 8912896 | tf_op jit(solution)/shard_map/all_gather | solution.py:37
  10.2 255.6 %all-gather.9.cloned.1.call-start = ((), (), s32[]{:S(2)}) async-start(), calls=%async_computation.2 | async-start | bytes 13369344 | tf_op jit(solution)/shard_map/all_gather | solution.py:34
  11.0 392.0 %all-reduce.3.cloned.1.call-start = ((), (), s32[]{:S(2)}) async-start(), calls=%async_computation | async-start | bytes 8388608 | tf_op jit(solution)/shard_map/psum | solution.py:49
  11.0 171.3 %collective-permute-start = (bf16[64,6,1024]{2,0,1:T(8,128)(2,1)}, bf16[64,6,1024]{2,0,1:T(8,128)(2,1)S(1)}, u32[]{:S(2)}, u32[]{:S(2)}) collective-permute-start(bf16[64,6,1024]{2,0,1:T(8,128)(2,1)} %bitcast.185), channel_id=1, source_target_pairs={{240,0},{0,16},{16,32},{32,48},{48,64},{64,80},{80,96},{96,112},{1... | collective-permute-start | bytes 2359304 | tf_op jit(solution)/shard_map/ppermute | solution.py:14
  14.1 264.6 %collective-permute-start.1 = (bf16[1024,1024]{1,0:T(8,128)(2,1)}, bf16[1024,1024]{1,0:T(8,128)(2,1)}, u32[]{:S(2)}, u32[]{:S(2)}) collective-permute-start(bf16[1024,1024]{1,0:T(8,128)(2,1)} %bitcast.184), channel_id=1, source_target_pairs={{240,0},{0,16},{16,32},{32,48},{48,64},{64,80},{80,96},{96,112},{1... | collective-permute-start | bytes 6291464 | tf_op jit(solution)/shard_map/ppermute | solution.py:14
  182.3 6.3 copy-start.4
  412.9 1.9 copy-start.2
  732.3 8.1 %copy-start.3 = (f32[8,128,128]{1,2,0:T(8,128)}, f32[8,128,128]{1,2,0:T(8,128)S(1)}, u32[]{:S(2)}) copy-start(f32[8,128,128]{1,2,0:T(8,128)S(1)} %custom-call.70) | copy-start | bytes 1572868
  740.8 9.1 %copy-start.1 = (bf16[1,1024,1024]{2,1,0:T(8,128)(2,1)S(1)}, bf16[1,1024,1024]{2,1,0:T(8,128)(2,1)}, u32[]{:S(2)}) copy-start(bf16[1,1024,1024]{2,1,0:T(8,128)(2,1)} %param.13) | copy-start | bytes 6291460
Sparse Core Ops, SparseCore 0:
  10.4 79.5 all-gather.6
  93.0 75.4 all-gather.10
  171.1 94.7 all-gather.8
  289.8 113.1 all-reduce.2
where the time goes:
time: 764 us; the launch traced here: 757 us
  waiting for transfers between devices  320 us (42%)
  other arithmetic  264 us (35%)
  matrix products  78.2 us (10%)
  local copies, waits for them, and re-layouts  71.6 us (9%)
  between operations  19.4 us (3%)
    another operation x30, other arithmetic, shards(): triangle = jnp.linalg.cholesky(correlation)  172 us
    psum x1, waiting for transfers between devices, shards(): correlation = lax.psum(local_correlation, 'bond')  112 us
    another operation x3, other arithmetic, shards(): solved = jax.scipy.linalg.solve_triangular(triangle, target.T, lower=True)  86.2 us
    all_gather x1, waiting for transfers between devices, shards(): current = lax.all_gather(cur_site[0], 'bond', axis=0, tiled=True)  75.9 us
    all_gather x1, waiting for transfers between devices, shards(): lax.all_gather(right_env[0], 'bond', axis=0, tiled=True)  65.7 us
    all_gather x1, waiting for transfers between devices, shards(): previous = lax.all_gather(prev_site[0], 'bond', axis=2, tiled=True)  64.7 us
    another operation x24, local copies, waits for them, and re-layouts  27.4 us
    another operation x14, matrix products, shards(): triangle = jnp.linalg.cholesky(correlation)  22.7 us
  transfers between devices with their start and end apart: 6, of which 4 were waited for; matrix products, arithmetic and copies ran while one was open for 8% of the time, Pallas kernels for 0%

commit v1 on v0

--- a/solution.py
+++ b/solution.py
@@ -6,6 +6,31 @@
 
 PHYS = 4
 MPOB = 6
+
+
+def joined_along(parts, dim):
+    lengths = list(parts.shape[1:])
+    lengths[dim] *= parts.shape[0]
+    return jnp.moveaxis(parts, 0, dim).reshape(lengths)
+
+
+def ring_apply(shard, axis, dim, apply, out_dim):
+    size, index, width = (lax.axis_size(axis), lax.axis_index(axis), shard.shape[dim])
+    forward = [(i, (i + 1) % size) for i in range(size)]
+    backward = [(i, (i - 1) % size) for i in range(size)]
+    half = size // 2
+    blocks = {}
+    from_left = from_right = shard
+    for step in range(half + 1):
+        next_left = lax.ppermute(from_left, axis, forward) if step < half else None
+        next_right = lax.ppermute(from_right, axis, backward) if step < size - half - 1 else None
+        blocks[-step] = apply(from_left, (index - step) % size * width)
+        if 0 < step < size - half:
+            blocks[step] = apply(from_right, (index + step) % size * width)
+        from_left, from_right = (next_left, next_right)
+    blocks = jnp.stack([blocks[k] for k in sorted(blocks)])
+    blocks = blocks[(jnp.arange(size) - index + half) % size]
+    return joined_along(blocks, out_dim)
 
 
 def shifted(block, axis, distance):
@@ -34,10 +59,15 @@
         lax.all_gather(right_env[0], "bond", axis=0, tiled=True),
         preferred_element_type=jnp.float32,
     )
-    previous = lax.all_gather(prev_site[0], "bond", axis=2, tiled=True)
     own_left = lax.dynamic_slice_in_dim(prev_now, lax.axis_index("bond") * own_rows, own_rows, 0)
-    partial_value = jnp.einsum(
-        "ab,bsc->asc", own_left, previous, preferred_element_type=jnp.float32
+    partial_value = ring_apply(
+        prev_site[0],
+        "bond",
+        2,
+        lambda part, offset_2: jnp.einsum(
+            "ab,bsc->asc", own_left, part, preferred_element_type=jnp.float32
+        ),
+        2,
     ).astype(jnp.bfloat16)
     second = jnp.einsum(
         "asc,cy->asy", partial_value, prev_right[0], preferred_element_type=jnp.float32

time: 764 us -> 740 us (0.969)
  waiting for transfers between devices: 320 us -> 182 us
  starting transfers between devices: 3.24 us -> 97.1 us
  matrix products: 78.2 us -> 104 us
  local copies, waits for them, and re-layouts: 71.6 us -> 62.8 us
    all_gather x1, waiting for transfers between devices: 75.9 us -> 0.01 us  [shards(): current = lax.all_gather(cur_site[0], 'bond', axis=0, tiled=True)]
    ppermute x0 -> x15, waiting for transfers between devices: none -> 66.4 us  [the longest x8 40.9 us: ring_apply(): next_left = lax.ppermute(from_left, axis, forward) if step < half else None]
    all_gather x1, waiting for transfers between devices: 65.7 us -> 0.01 us  [shards(): lax.all_gather(right_env[0], 'bond', axis=0, tiled=True)]
    all_gather x1 -> x0, waiting for transfers between devices: 64.7 us -> none  [shards(): previous = lax.all_gather(prev_site[0], 'bond', axis=2, tiled=True)]
    ppermute x2, starting transfers between devices: 3.08 us -> 58.2 us  [shifted(): return lax.ppermute(block, axis, route)]
    ppermute x0 -> x15, starting transfers between devices: none -> 38.8 us  [the longest x7 36.5 us: ring_apply(): lax.ppermute(from_right, axis, backward)]
    dot_general x0 -> x16, matrix products: none -> 32.2 us  [shards(): jnp.einsum('ab,bsc->asc', own_left, part, preferred_element_type=jnp.floa...]
    all_gather x1 -> x0, local copies, waits for them, and re-layouts: 13.7 us -> none  [shards(): previous = lax.all_gather(prev_site[0], 'bond', axis=2, tiled=True)]
  transfers between devices with their start and end apart: 6 -> 20, of which waited for: 4 -> 9; matrix products, arithmetic and copies ran while one was open for 8% -> 10% of each run, Pallas kernels for 0% -> 0%
where the time goes in v1:
time: 740 us; the launch traced here: 730 us
  other arithmetic  265 us (36%)
  waiting for transfers between devices  182 us (25%)
  matrix products  104 us (14%)
  starting transfers between devices  97.1 us (13%)
  local copies, waits for them, and re-layouts  62.8 us (8%)
  between operations  19.6 us (3%)
    another operation x30, other arithmetic, shards(): triangle = jnp.linalg.cholesky(correlation)  173 us
    psum x1, waiting for transfers between devices, shards(): correlation = lax.psum(local_correlation, 'bond')  114 us
    another operation x3, other arithmetic, shards(): solved = jax.scipy.linalg.solve_triangular(triangle, target.T, lower=True)  86.2 us
    ppermute x2, starting transfers between devices, shifted(): return lax.ppermute(block, axis, route)  58.2 us
    ppermute x8, waiting for transfers between devices, ring_apply(): next_left = lax.ppermute(from_left, axis, forward) if step < half else None  40.9 us
    ppermute x7, starting transfers between devices, ring_apply(): lax.ppermute(from_right, axis, backward)  36.5 us
    dot_general x16, matrix products, shards(): jnp.einsum('ab,bsc->asc', own_left, part, preferred_element_type=jnp.floa...  32.2 us
    another operation x24, local copies, waits for them, and re-layouts  27.3 us
  transfers between devices with their start and end apart: 20, of which 9 were waited for; matrix products, arithmetic and copies ran while one was open for 10% of the time, Pallas kernels for 0%

profile of v1, /device:TPU:1, one launch (start us, length us, event | category | flops | bytes accessed | tf_op | source)
XLA Modules:
  0.0 729.9 jit_solution(16306014919667298672)
XLA Ops:
  10.9 13.5 %collective-permute-done.2 = bf16[1024,4,64]{0,2,1:T(8,128)(2,1)S(1)} collective-permute-done((bf16[1024,4,64]{0,2,1:T(8,128)(2,1)}, bf16[1024,4,64]{0,2,1:T(8,128)(2,1)S(1)}, u32[]{:S(2)}, u32[]{:S(2)}) %collective-permute-start.2) | collective-permute-done | bytes 524320 | tf_op jit(solution)/shard_map/ppermute | solution.py:25
  29.2 15.1 %collective-permute-done.3 = bf16[1024,4,64]{0,2,1:T(8,128)(2,1)S(1)} collective-permute-done((bf16[1024,4,64]{0,2,1:T(8,128)(2,1)S(1)}, bf16[1024,4,64]{0,2,1:T(8,128)(2,1)S(1)}, u32[]{:S(2)}, u32[]{:S(2)}) %collective-permute-start.3) | collective-permute-done | bytes 524320 | tf_op jit(solution)/shard_map/ppermute | solution.py:25
  68.0 31.2 %collective-permute-start.1 = (bf16[1024,1024]{1,0:T(8,128)(2,1)}, bf16[1024,1024]{1,0:T(8,128)(2,1)}, u32[]{:S(2)}, u32[]{:S(2)}) collective-permute-start(bf16[1024,1024]{1,0:T(8,128)(2,1)} %bitcast.301), channel_id=1, source_target_pairs={{240,0},{0,16},{16,32},{32,48},{48,64},{64,80},{80,96},{96,112},{1... | collective-permute-start | bytes 6291464 | tf_op jit(solution)/shard_map/ppermute | solution.py:39
  104.5 14.7 %collective-permute-done.13 = bf16[1024,4,64]{0,2,1:T(8,128)(2,1)S(1)} collective-permute-done((bf16[1024,4,64]{0,2,1:T(8,128)(2,1)S(1)}, bf16[1024,4,64]{0,2,1:T(8,128)(2,1)S(1)}, u32[]{:S(2)}, u32[]{:S(2)}) %collective-permute-start.13) | collective-permute-done | bytes 524320 | tf_op jit(solution)/shard_map/ppermute | solution.py:26
  125.1 10.0 %collective-permute-done.14 = bf16[1024,4,64]{0,2,1:T(8,128)(2,1)} collective-permute-done((bf16[1024,4,64]{0,2,1:T(8,128)(2,1)S(1)}, bf16[1024,4,64]{0,2,1:T(8,128)(2,1)}, u32[]{:S(2)}, u32[]{:S(2)}) %collective-permute-start.14) | collective-permute-done | bytes 524320 | tf_op jit(solution)/shard_map/ppermute | solution.py:26
  140.4 26.9 %collective-permute-start = (bf16[64,6,1024]{2,0,1:T(8,128)(2,1)}, bf16[64,6,1024]{2,0,1:T(8,128)(2,1)}, u32[]{:S(2)}, u32[]{:S(2)}) collective-permute-start(bf16[64,6,1024]{2,0,1:T(8,128)(2,1)} %bitcast.302), channel_id=1, source_target_pairs={{240,0},{0,16},{16,32},{32,48},{48,64},{64,80},{80,96},{96,112},{1... | collective-permute-start | bytes 2359304 | tf_op jit(solution)/shard_map/ppermute | solution.py:39
  211.6 13.9 %copy.63 = bf16[1,1024,4,1024]{1,3,2,0:T(8,128)(2,1)} copy(bf16[1,1024,4,1024]{3,2,0,1:T(4,128)(2,1)} %all-gather.5.cloned.1.call-done) | data formatting | bytes 16777216 | tf_op jit(solution)/shard_map/reshape | solution.py:50
  231.6 11.0 %fusion.6 = bf16[64,4,6,1024]{3,2,1,0:T(8,128)(2,1)} fusion(f32[64,6,4,1024,1]{3,0,2,1,4:T(8,128)S(1)} %fusion.12, bf16[1,6,6,4,4]{2,4,3,1,0:T(4,128)(2,1)S(1)} %copy-done.20), kind=kOutput, calls=%fused_computation.10 | convolution fusion | flops 454557696 | bytes 9438336 | tf_op jit(solution)/shard_map/autc,uvst->asvc/dot_general | solution.py:53
  242.6 11.6 %fusion.22 = f32[64,4,1024]{2,0,1:T(8,128)S(1)} fusion(bf16[1,1024,6,1024]{3,1,2,0:T(8,128)(2,1)} %all-gather.7.cloned.1.call-done, bf16[64,4,6,1024]{3,2,1,0:T(8,128)(2,1)} %fusion.6), kind=kOutput, calls=%fused_computation.22 | convolution fusion | flops 3221487616 | bytes 16777216 | tf_op jit(solution)/shard_map/asvc,cvy->asy/dot_general | solution.py:56
  261.8 114.1 %all-reduce.3.cloned.1.call-done = f32[1024,1024]{0,1:T(8,128)} async-done(((f32[1024,1024]{0,1:T(8,128)}), f32[1024,1024]{0,1:T(8,128)}) %all-reduce.3.cloned.1.call-update) | async-done | bytes 4194320 | tf_op jit(solution)/shard_map/psum | solution.py:79
  387.7 11.7 %cholesky.223 = f32[128,128]{1,0:T(8,128)S(1)} custom-call(f32[128,128]{1,0:T(8,128)S(1)} %cholesky.580), custom_call_target="Cholesky" | custom-call | tf_op jit(solution)/shard_map/jit(cholesky)/cholesky | solution.py:80
  399.5 9.8 %custom-call.63 = f32[1,128,128]{1,2,0:T(8,128)S(1)} custom-call(f32[1,128,128]{2,1,0:T(8,128)S(1)} %get-tuple-element.74), custom_call_target="InvertDiagBlocksLowerTriangular" | custom-call | tf_op jit(solution)/shard_map/jit(cholesky)/cholesky | solution.py:80
  415.5 12.1 %cholesky.244 = f32[128,128]{1,0:T(8,128)S(1)} custom-call(f32[128,128]{1,0:T(8,128)S(1)} %cholesky.584), custom_call_target="Cholesky" | custom-call | tf_op jit(solution)/shard_map/jit(cholesky)/cholesky | solution.py:80
  429.1 9.8 %custom-call.64 = f32[1,128,128]{1,2,0:T(8,128)S(1)} custom-call(f32[1,128,128]{2,1,0:T(8,128)S(1)} %get-tuple-element.71), custom_call_target="InvertDiagBlocksLowerTriangular" | custom-call | tf_op jit(solution)/shard_map/jit(cholesky)/cholesky | solution.py:80
  442.3 11.7 %cholesky.468 = f32[128,128]{1,0:T(8,128)S(1)} custom-call(f32[128,128]{1,0:T(8,128)S(1)} %cholesky.589), custom_call_target="Cholesky" | custom-call | tf_op jit(solution)/shard_map/jit(cholesky)/cholesky | solution.py:80
  468.7 11.9 %cholesky.487 = f32[128,128]{1,0:T(8,128)S(1)} custom-call(f32[128,128]{1,0:T(8,128)S(1)} %cholesky.594), custom_call_target="Cholesky" | custom-call | tf_op jit(solution)/shard_map/jit(cholesky)/cholesky | solution.py:80
  495.2 11.7 %cholesky.506 = f32[128,128]{1,0:T(8,128)S(1)} custom-call(f32[128,128]{1,0:T(8,128)S(1)} %cholesky.599), custom_call_target="Cholesky" | custom-call | tf_op jit(solution)/shard_map/jit(cholesky)/cholesky | solution.py:80
  508.2 10.0 %custom-call.67 = f32[1,128,128]{1,2,0:T(8,128)S(1)} custom-call(f32[1,128,128]{2,1,0:T(8,128)S(1)} %get-tuple-element.62), custom_call_target="InvertDiagBlocksLowerTriangular" | custom-call | tf_op jit(solution)/shard_map/jit(cholesky)/cholesky | solution.py:80
  521.5 11.7 %cholesky.526 = f32[128,128]{1,0:T(8,128)S(1)} custom-call(f32[128,128]{1,0:T(8,128)S(1)} %cholesky.604), custom_call_target="Cholesky" | custom-call | tf_op jit(solution)/shard_map/jit(cholesky)/cholesky | solution.py:80
  547.3 12.1 %cholesky.546 = f32[128,128]{1,0:T(8,128)S(1)} custom-call(f32[128,128]{1,0:T(8,128)S(1)} %cholesky.609), custom_call_target="Cholesky" | custom-call | tf_op jit(solution)/shard_map/jit(cholesky)/cholesky | solution.py:80
  560.7 9.8 %custom-call.69 = f32[1,128,128]{1,2,0:T(8,128)S(1)} custom-call(f32[1,128,128]{2,1,0:T(8,128)S(1)} %get-tuple-element.56), custom_call_target="InvertDiagBlocksLowerTriangular" | custom-call | tf_op jit(solution)/shard_map/jit(cholesky)/cholesky | solution.py:80
  573.2 11.7 %cholesky.564 = f32[128,128]{1,0:T(8,128)S(1)} custom-call(f32[128,128]{1,0:T(8,128)S(1)} %convolution_subtract_fusion.13), custom_call_target="Cholesky" | custom-call | tf_op jit(solution)/shard_map/jit(cholesky)/cholesky | solution.py:80
  598.7 27.4 %while.1 = (s32[]{:T(128)}, f32[1024,1024]{1,0:T(8,128)}, s32[8,2]{0,1:T(2,128)S(1)}, f32[8,128,128]{2,1,0:T(8,128)}, s32[]{:T(128)}) while((s32[]{:T(128)}, f32[1024,1024]{1,0:T(8,128)}, s32[8,2]{0,1:T(2,128)S(1)}, f32[8,128,128]{2,1,0:T(8,128)}, s32[]{:T(128)}) %tuple.64), condition=%wide.while_cond, body=%wide.while_body.sunk | while | flops 2 | bytes 132705 | solution.py:81
  626.1 79.6 %custom-call.70 = f32[8,128,128]{1,2,0:T(8,128)S(1)} custom-call(f32[8,128,128]{2,1,0:T(8,128)} %get-tuple-element.9), custom_call_target="InvertDiagBlocksLowerTriangular" | custom-call | tf_op jit(solution)/shard_map/jit(_solve_triangular)/triangular_solve | solution.py:81
  (197 shorter events, 234.4 us)
Async XLA Ops:
  7.2 247.1 %copy-start = (bf16[1,1024,1024]{2,1,0:T(8,128)(2,1)S(1)}, bf16[1,1024,1024]{2,1,0:T(8,128)(2,1)}, u32[]{:S(2)}) copy-start(bf16[1,1024,1024]{2,1,0:T(8,128)(2,1)} %param.13) | copy-start | bytes 6291460
  7.2 182.5 %copy-start.4 = (bf16[1,1024,4,64]{1,3,2,0:T(8,128)(2,1)S(1)}, bf16[1,1024,4,64]{1,3,2,0:T(8,128)(2,1)}, u32[]{:S(2)}) copy-start(bf16[1,1024,4,64]{1,3,2,0:T(8,128)(2,1)} %param.10) | copy-start | bytes 1572868
  7.2 204.4 %all-gather.5.cloned.1.call-start = ((), (), s32[]{:S(2)}) async-start(), calls=%async_computation.1 | async-start | bytes 8912896 | tf_op jit(solution)/shard_map/all_gather | solution.py:47
  7.9 234.7 %all-gather.7.cloned.1.call-start = ((), (), s32[]{:S(2)}) async-start(), calls=%async_computation.2 | async-start | bytes 13369344 | tf_op jit(solution)/shard_map/all_gather | solution.py:59
  8.7 367.3 %all-reduce.3.cloned.1.call-start = ((), (), s32[]{:S(2)}) async-start(), calls=%async_computation | async-start | bytes 8388608 | tf_op jit(solution)/shard_map/psum | solution.py:79
  8.7 15.7 %collective-permute-start.2 = (bf16[1024,4,64]{0,2,1:T(8,128)(2,1)}, bf16[1024,4,64]{0,2,1:T(8,128)(2,1)S(1)}, u32[]{:S(2)}, u32[]{:S(2)}) collective-permute-start(bf16[1024,4,64]{0,2,1:T(8,128)(2,1)} %bitcast.298), channel_id=1, source_target_pairs={{0,1},{1,2},{2,3},{3,4},{4,5},{5,6},{6,7},{7,8},{8,9},{9,10},{10,1... | collective-permute-start | bytes 1572872 | tf_op jit(solution)/shard_map/ppermute | solution.py:25
  24.5 19.9 %collective-permute-start.3 = (bf16[1024,4,64]{0,2,1:T(8,128)(2,1)S(1)}, bf16[1024,4,64]{0,2,1:T(8,128)(2,1)S(1)}, u32[]{:S(2)}, u32[]{:S(2)}) collective-permute-start(bf16[1024,4,64]{0,2,1:T(8,128)(2,1)S(1)} %collective-permute-done.2), channel_id=1, source_target_pairs={{0,1},{1,2},{2,3},{3,4},{4,5},{5,6},{6,7},{7,8},{8,9},{9,10},{10,1... | collective-permute-start | bytes 1572872 | tf_op jit(solution)/shard_map/ppermute | solution.py:25
  24.5 19.9 %collective-permute-start.10 = (bf16[1024,4,64]{0,2,1:T(8,128)(2,1)}, bf16[1024,4,64]{0,2,1:T(8,128)(2,1)S(1)}, u32[]{:S(2)}, u32[]{:S(2)}) collective-permute-start(bf16[1024,4,64]{0,2,1:T(8,128)(2,1)} %bitcast.299), channel_id=1, source_target_pairs={{0,15},{1,0},{2,1},{3,2},{4,3},{5,4},{6,5},{7,6},{8,7},{9,8},{10,9... | collective-permute-start | bytes 1572872 | tf_op jit(solution)/shard_map/ppermute | solution.py:26
  44.4 11.4 %collective-permute-start.4 = (bf16[1024,4,64]{0,2,1:T(8,128)(2,1)S(1)}, bf16[1024,4,64]{0,2,1:T(8,128)(2,1)S(1)}, u32[]{:S(2)}, u32[]{:S(2)}) collective-permute-start(bf16[1024,4,64]{0,2,1:T(8,128)(2,1)S(1)} %collective-permute-done.3), channel_id=1, source_target_pairs={{0,1},{1,2},{2,3},{3,4},{4,5},{5,6},{6,7},{7,8},{8,9},{9,10},{10,1... | collective-permute-start | bytes 1572872 | tf_op jit(solution)/shard_map/ppermute | solution.py:25
  45.2 11.3 %collective-permute-start.11 = (bf16[1024,4,64]{0,2,1:T(8,128)(2,1)S(1)}, bf16[1024,4,64]{0,2,1:T(8,128)(2,1)S(1)}, u32[]{:S(2)}, u32[]{:S(2)}) collective-permute-start(bf16[1024,4,64]{0,2,1:T(8,128)(2,1)S(1)} %collective-permute-done.10), channel_id=1, source_target_pairs={{0,15},{1,0},{2,1},{3,2},{4,3},{5,4},{6,5},{7,6},{8,7},{9,8},{10,9... | collective-permute-start | bytes 1572872 | tf_op jit(solution)/shard_map/ppermute | solution.py:26
  55.7 43.5 %copy-start.11 = (bf16[1024,4,64]{0,2,1:T(8,128)(2,1)}, bf16[1024,4,64]{0,2,1:T(8,128)(2,1)S(1)}, u32[]{:S(2)}) copy-start(bf16[1024,4,64]{0,2,1:T(8,128)(2,1)S(1)} %collective-permute-done.4) | copy-start | bytes 1572868
  55.7 12.3 %collective-permute-start.5 = (bf16[1024,4,64]{0,2,1:T(8,128)(2,1)S(1)}, bf16[1024,4,64]{0,2,1:T(8,128)(2,1)S(1)}, u32[]{:S(2)}, u32[]{:S(2)}) collective-permute-start(bf16[1024,4,64]{0,2,1:T(8,128)(2,1)S(1)} %collective-permute-done.4), channel_id=1, source_target_pairs={{0,1},{1,2},{2,3},{3,4},{4,5},{5,6},{6,7},{7,8},{8,9},{9,10},{10,1... | collective-permute-start | bytes 1572872 | tf_op jit(solution)/shard_map/ppermute | solution.py:25
  56.5 42.7 %collective-permute-start.12 = (bf16[1024,4,64]{0,2,1:T(8,128)(2,1)S(1)}, bf16[1024,4,64]{0,2,1:T(8,128)(2,1)S(1)}, u32[]{:S(2)}, u32[]{:S(2)}) collective-permute-start(bf16[1024,4,64]{0,2,1:T(8,128)(2,1)S(1)} %collective-permute-done.11), channel_id=1, source_target_pairs={{0,15},{1,0},{2,1},{3,2},{4,3},{5,4},{6,5},{7,6},{8,7},{9,8},{10,9... | collective-permute-start | bytes 1572872 | tf_op jit(solution)/shard_map/ppermute | solution.py:26
  68.0 51.2 %copy-start.14 = (bf16[1024,4,64]{0,2,1:T(8,128)(2,1)}, bf16[1024,4,64]{0,2,1:T(8,128)(2,1)S(1)}, u32[]{:S(2)}) copy-start(bf16[1024,4,64]{0,2,1:T(8,128)(2,1)S(1)} %collective-permute-done.5) | copy-start | bytes 1572868
  68.0 36.4 %collective-permute-start.6 = (bf16[1024,4,64]{0,2,1:T(8,128)(2,1)S(1)}, bf16[1024,4,64]{0,2,1:T(8,128)(2,1)S(1)}, u32[]{:S(2)}, u32[]{:S(2)}) collective-permute-start(bf16[1024,4,64]{0,2,1:T(8,128)(2,1)S(1)} %collective-permute-done.5), channel_id=1, source_target_pairs={{0,1},{1,2},{2,3},{3,4},{4,5},{5,6},{6,7},{7,8},{8,9},{9,10},{10,1... | collective-permute-start | bytes 1572872 | tf_op jit(solution)/shard_map/ppermute | solution.py:25
  68.0 105.0 %collective-permute-start.1 = (bf16[1024,1024]{1,0:T(8,128)(2,1)}, bf16[1024,1024]{1,0:T(8,128)(2,1)}, u32[]{:S(2)}, u32[]{:S(2)}) collective-permute-start(bf16[1024,1024]{1,0:T(8,128)(2,1)} %bitcast.301), channel_id=1, source_target_pairs={{240,0},{0,16},{16,32},{32,48},{48,64},{64,80},{80,96},{96,112},{1... | collective-permute-start | bytes 6291464 | tf_op jit(solution)/shard_map/ppermute | solution.py:39
  99.3 19.9 %collective-permute-start.13 = (bf16[1024,4,64]{0,2,1:T(8,128)(2,1)S(1)}, bf16[1024,4,64]{0,2,1:T(8,128)(2,1)S(1)}, u32[]{:S(2)}, u32[]{:S(2)}) collective-permute-start(bf16[1024,4,64]{0,2,1:T(8,128)(2,1)S(1)} %collective-permute-done.12), channel_id=1, source_target_pairs={{0,15},{1,0},{2,1},{3,2},{4,3},{5,4},{6,5},{7,6},{8,7},{9,8},{10,9... | collective-permute-start | bytes 1572872 | tf_op jit(solution)/shard_map/ppermute | solution.py:26
  104.4 20.7 %collective-permute-start.7 = (bf16[1024,4,64]{0,2,1:T(8,128)(2,1)S(1)}, bf16[1024,4,64]{0,2,1:T(8,128)(2,1)S(1)}, u32[]{:S(2)}, u32[]{:S(2)}) collective-permute-start(bf16[1024,4,64]{0,2,1:T(8,128)(2,1)S(1)} %collective-permute-done.6), channel_id=1, source_target_pairs={{0,1},{1,2},{2,3},{3,4},{4,5},{5,6},{6,7},{7,8},{8,9},{9,10},{10,1... | collective-permute-start | bytes 1572872 | tf_op jit(solution)/shard_map/ppermute | solution.py:25
  119.2 15.9 %collective-permute-start.14 = (bf16[1024,4,64]{0,2,1:T(8,128)(2,1)S(1)}, bf16[1024,4,64]{0,2,1:T(8,128)(2,1)}, u32[]{:S(2)}, u32[]{:S(2)}) collective-permute-start(bf16[1024,4,64]{0,2,1:T(8,128)(2,1)S(1)} %collective-permute-done.13), channel_id=1, source_target_pairs={{0,15},{1,0},{2,1},{3,2},{4,3},{5,4},{6,5},{7,6},{8,7},{9,8},{10,9... | collective-permute-start | bytes 1572872 | tf_op jit(solution)/shard_map/ppermute | solution.py:26
  125.1 15.4 %collective-permute-start.8 = (bf16[1024,4,64]{0,2,1:T(8,128)(2,1)S(1)}, bf16[1024,4,64]{0,2,1:T(8,128)(2,1)}, u32[]{:S(2)}, u32[]{:S(2)}) collective-permute-start(bf16[1024,4,64]{0,2,1:T(8,128)(2,1)S(1)} %collective-permute-done.7), channel_id=1, source_target_pairs={{0,1},{1,2},{2,3},{3,4},{4,5},{5,6},{6,7},{7,8},{8,9},{9,10},{10,1... | collective-permute-start | bytes 1572872 | tf_op jit(solution)/shard_map/ppermute | solution.py:25
  135.1 32.3 %collective-permute-start.15 = (bf16[1024,4,64]{0,2,1:T(8,128)(2,1)}, bf16[1024,4,64]{0,2,1:T(8,128)(2,1)}, u32[]{:S(2)}, u32[]{:S(2)}) collective-permute-start(bf16[1024,4,64]{0,2,1:T(8,128)(2,1)} %collective-permute-done.14), channel_id=1, source_target_pairs={{0,15},{1,0},{2,1},{3,2},{4,3},{5,4},{6,5},{7,6},{8,7},{9,8},{10,9... | collective-permute-start | bytes 1572872 | tf_op jit(solution)/shard_map/ppermute | solution.py:26
  140.4 32.6 %collective-permute-start.9 = (bf16[1024,4,64]{0,2,1:T(8,128)(2,1)}, bf16[1024,4,64]{0,2,1:T(8,128)(2,1)}, u32[]{:S(2)}, u32[]{:S(2)}) collective-permute-start(bf16[1024,4,64]{0,2,1:T(8,128)(2,1)} %collective-permute-done.8), channel_id=1, source_target_pairs={{0,1},{1,2},{2,3},{3,4},{4,5},{5,6},{6,7},{7,8},{8,9},{9,10},{10,1... | collective-permute-start | bytes 1572872 | tf_op jit(solution)/shard_map/ppermute | solution.py:25
  140.4 85.1 %collective-permute-start = (bf16[64,6,1024]{2,0,1:T(8,128)(2,1)}, bf16[64,6,1024]{2,0,1:T(8,128)(2,1)}, u32[]{:S(2)}, u32[]{:S(2)}) collective-permute-start(bf16[64,6,1024]{2,0,1:T(8,128)(2,1)} %bitcast.302), channel_id=1, source_target_pairs={{240,0},{0,16},{16,32},{32,48},{48,64},{64,80},{80,96},{96,112},{1... | collective-permute-start | bytes 2359304 | tf_op jit(solution)/shard_map/ppermute | solution.py:39
  167.4 36.0 %collective-permute-start.16 = (bf16[1024,4,64]{0,2,1:T(8,128)(2,1)}, bf16[1024,4,64]{0,2,1:T(8,128)(2,1)S(1)}, u32[]{:S(2)}, u32[]{:S(2)}) collective-permute-start(bf16[1024,4,64]{0,2,1:T(8,128)(2,1)} %collective-permute-done.15), channel_id=1, source_target_pairs={{0,15},{1,0},{2,1},{3,2},{4,3},{5,4},{6,5},{7,6},{8,7},{9,8},{10,9... | collective-permute-start | bytes 1572872 | tf_op jit(solution)/shard_map/ppermute | solution.py:26
  (17 other events, 230.4 us)
Sparse Core Ops, SparseCore 0:
  10.5 112.2 all-gather.4
  125.2 109.1 all-gather.6
  260.5 115.3 all-reduce.2
